TPU v7x, 256 devices: a whole 4x4x8 slice. The times are simulated.
256 devices in a mesh: row: 8 (over z_lo, y), col: 32 (over z_hi, x, core).
Axes of the slice: x: 4, y: 4, z: 8 (z_hi: 4, z_lo: 2; z = z_hi * 2 + z_lo), core: 2. Of those that a mesh axis runs over, the one named last changes fastest.
Arguments:
- activations: bfloat16 [1024, 8192], P('col', 'row'), may hold values from -6 to 6
- cotangent: bfloat16 [1024, 8192], P('col', 'row'), may hold values from -0.59765625 to 0.59765625
- gate_weight: bfloat16 [8192, 21504], P('row', 'col'), may hold values from -0.0625 to 0.0625
- up_weight: bfloat16 [8192, 21504], P('row', 'col'), may hold values from -0.0625 to 0.0625
- down_weight: bfloat16 [21504, 8192], P('col', 'row'), may hold values from -0.0390625 to 0.0390625
Outputs:
- input_grad: bfloat16 [1024, 8192], P('col', 'row')
- gate_grad: bfloat16 [8192, 21504], P('row', 'col')
- up_grad: bfloat16 [8192, 21504], P('row', 'col')
- down_grad: bfloat16 [21504, 8192], P('col', 'row')
All inputs are finite; a program needn't handle non-finite values.
Results may differ from a plain program's by a relative error of at most 0.005.
Values may be sent and summed in bfloat16 or wider, within the bound.
No kernel may reach another device: no remote copies, remote signals or barrier semaphores. Data moves between devices by JAX's collectives and lax.ppermute only.
A program may use at most 128 MiB of HBM per device.

v0:
```python
import jax
import jax.numpy as jnp
from jax import lax
from jax.sharding import PartitionSpec as P


def local_deltas(sums, hid_cols):
    gate = sums[:, :hid_cols]
    up = sums[:, hid_cols : 2 * hid_cols]
    hidden_grad = sums[:, 2 * hid_cols :]
    sigmoid_gate = jax.nn.sigmoid(gate)
    hidden = (gate * sigmoid_gate * up).astype(jnp.bfloat16)
    gate_delta = (hidden_grad * up * sigmoid_gate * (1.0 + gate * (1.0 - sigmoid_gate))).astype(
        jnp.bfloat16
    )
    up_delta = (hidden_grad * gate * sigmoid_gate).astype(jnp.bfloat16)
    return (hidden, gate_delta, up_delta)


def per_device(activations, cotangent, gate_weight, up_weight, down_weight):
    act_all, cot_all = (
        lax.all_gather(activations, "col", axis=0, tiled=True),
        lax.all_gather(cotangent, "col", axis=0, tiled=True),
    )
    hid_cols = gate_weight.shape[1]
    both_weights = jnp.concatenate([gate_weight, up_weight], axis=1)
    contract_cols = (((1,), (1,)), ((), ()))
    contract_rows = (((0,), (0,)), ((), ()))
    forward_part = jnp.dot(act_all, both_weights, preferred_element_type=jnp.float32)
    backward_part = lax.dot_general(
        cot_all, down_weight, contract_cols, preferred_element_type=jnp.float32
    )
    sums = lax.psum_scatter(
        jnp.concatenate([forward_part, backward_part], axis=1),
        "row",
        scatter_dimension=0,
        tiled=True,
    )
    hidden, gate_delta, up_delta = local_deltas(sums, hid_cols)
    hidden, gate_delta, up_delta = (
        lax.all_gather(hidden, "row", axis=0, tiled=True),
        lax.all_gather(gate_delta, "row", axis=0, tiled=True),
        lax.all_gather(up_delta, "row", axis=0, tiled=True),
    )
    down_grad = lax.dot_general(
        hidden, cot_all, contract_rows, preferred_element_type=jnp.float32
    ).astype(jnp.bfloat16)
    gate_grad = lax.dot_general(
        act_all, gate_delta, contract_rows, preferred_element_type=jnp.float32
    ).astype(jnp.bfloat16)
    up_grad = lax.dot_general(
        act_all, up_delta, contract_rows, preferred_element_type=jnp.float32
    ).astype(jnp.bfloat16)
    both_deltas = jnp.concatenate([gate_delta, up_delta], axis=1)
    input_grad = lax.psum_scatter(
        lax.dot_general(
            both_deltas, both_weights, contract_cols, preferred_element_type=jnp.float32
        ),
        "col",
        scatter_dimension=0,
        tiled=True,
    )
    return (input_grad.astype(jnp.bfloat16), gate_grad, up_grad, down_grad)


def solution(mesh):
    return jax.shard_map(
        per_device,
        mesh=mesh,
        in_specs=(
            P("col", "row"),
            P("col", "row"),
            P("row", "col"),
            P("row", "col"),
            P("col", "row"),
        ),
        out_specs=(P("col", "row"), P("row", "col"), P("row", "col"), P("col", "row")),
        check_vma=False,
    )
```

profile of v0, /device:TPU:8, one launch (start us, length us, event | category | flops | bytes accessed | tf_op | source)
XLA Modules:
  0.0 472.7 jit_solution(8116359554584954687)
XLA Ops:
  7.2 0.0 copy-start
  7.2 0.0 copy-start.2
  7.2 0.0 all-gather.8.cloned.1.call-start
  7.2 0.7 all-gather.8.cloned.1.call-update
  7.9 0.0 all-gather.6.cloned.1.call-start
  8.0 0.7 all-gather.6.cloned.1.call-update
  8.7 0.0 reduce-scatter.3.cloned.1.call-start
  8.7 2.6 constant_dynamic-update-slice_fusion.1
  11.3 0.0 copy-done.2
  11.3 1.2 constant_dynamic-update-slice_fusion
  12.5 55.7 %all-gather.8.cloned.1.call-done = bf16[1024,1024]{1,0:T(8,128)(2,1)} async-done(((bf16[32,1024]{1,0:T(8,128)(2,1)}), bf16[1024,1024]{1,0:T(8,128)(2,1)}) %all-gather.8.cloned.1.call-update) | async-done | bytes 2097168 | tf_op jit(solution)/shard_map/all_gather | solution.py:23
  68.2 0.0 copy-done
  68.2 4.8 %fusion.7 = f32[1024,672]{0,1:T(8,128)} fusion(bf16[1024,1024]{1,0:T(8,128)(2,1)} %all-gather.8.cloned.1.call-done, bf16[672,1024]{1,0:T(8,128)(2,1)S(1)} %copy-done), kind=kOutput, calls=%fused_computation.18 | convolution fusion | flops 1409286144 | bytes 6225920 | tf_op jit(solution)/shard_map/dot_general | solution.py:30
  73.0 49.5 %all-gather.6.cloned.1.call-done = bf16[1024,1024]{1,0:T(8,128)(2,1)} async-done(((bf16[32,1024]{1,0:T(8,128)(2,1)}), bf16[1024,1024]{1,0:T(8,128)(2,1)}) %all-gather.6.cloned.1.call-update) | async-done | bytes 2097168 | tf_op jit(solution)/shard_map/all_gather | solution.py:22
  122.4 0.0 copy-start.1
  122.4 5.6 %convolution_bitcast_fusion = f32[1024,1344]{0,1:T(8,128)S(1)} fusion(bf16[1024,1344]{0,1:T(8,128)(2,1)} %constant_dynamic-update-slice_fusion, bf16[1024,1024]{1,0:T(8,128)(2,1)} %all-gather.6.cloned.1.call-done), kind=kOutput, calls=%fused_computation.1 | convolution fusion | flops 2818572288 | bytes 10354688 | tf_op jit(solution)/shard_map/dot_general | solution.py:29
  128.1 0.0 copy-done.1
  128.1 4.9 %pad_maximum_fusion = f32[1024,2016]{0,1:T(8,128)} fusion(f32[1024,672]{0,1:T(8,128)S(1)} %copy-done.1, f32[1024,1344]{0,1:T(8,128)S(1)} %convolution_bitcast_fusion), kind=kLoop, calls=%fused_computation | loop fusion | flops 2064384 | bytes 16515072 | tf_op jit(solution)/shard_map/concatenate | solution.py:34
  133.0 0.0 reduce-scatter.3.cloned.1.call-update
  133.0 0.0 all-gather.10.cloned.1.call-start
  133.1 89.0 %reduce-scatter.3.cloned.1.call-done = f32[128,2016]{0,1:T(8,128)} async-done(((f32[1024,2016]{0,1:T(8,128)}), f32[128,2016]{0,1:T(8,128)}) %reduce-scatter.3.cloned.1.call-update) | async-done | bytes 1032208 | tf_op jit(solution)/shard_map/reduce_scatter | solution.py:33
  222.0 2.1 multiply_convert_fusion
  224.1 0.0 all-gather.10.cloned.1.call-update
  224.2 0.0 all-gather.12.cloned.1.call-start
  224.2 0.5 all-gather.12.cloned.1.call-update
  224.8 0.0 all-gather.14.cloned.1.call-start
  224.8 0.5 all-gather.14.cloned.1.call-update
  225.3 0.2 reduce-scatter.5.cloned.1.call-start
  225.6 41.6 %all-gather.10.cloned.1.call-done = bf16[1024,672]{0,1:T(8,128)(2,1)} async-done(((bf16[128,672]{0,1:T(8,128)(2,1)}), bf16[1024,672]{0,1:T(8,128)(2,1)}) %all-gather.10.cloned.1.call-update) | async-done | bytes 1376272 | tf_op jit(solution)/shard_map/all_gather | solution.py:42
  267.2 45.7 %all-gather.12.cloned.1.call-done = bf16[1024,672]{0,1:T(8,128)(2,1)} async-done(((bf16[128,672]{0,1:T(8,128)(2,1)}), bf16[1024,672]{0,1:T(8,128)(2,1)}) %all-gather.12.cloned.1.call-update) | async-done | bytes 1376272 | tf_op jit(solution)/shard_map/all_gather | solution.py:43
  312.9 8.2 %fusion = f32[1024,1024]{1,0:T(8,128)} fusion(bf16[1024,1344]{0,1:T(8,128)(2,1)} %constant_dynamic-update-slice_fusion, bf16[1024,672]{0,1:T(8,128)(2,1)} %all-gather.12.cloned.1.call-done, bf16[1024,672]{0,1:T(8,128)(2,1)} %all-gather.10.cloned.1.call-done), kind=kOutput, calls=%fused_computation.2 | convolution fusion | flops 2824077312 | bytes 9699328 | tf_op jit(solution)/shard_map/dot_general | solution.py:56
  321.0 0.0 copy-start.4
  321.0 0.0 reduce-scatter.5.cloned.1.call-update
  321.1 1.6 copy-done.4
  322.6 0.0 copy-start.5
  322.6 0.0 copy-start.6
  322.6 4.2 fusion.5
  326.8 0.0 copy-done.5
  326.8 0.0 copy-done.6
  326.8 0.0 copy-start.3
  326.8 2.7 fusion.4
  329.5 29.1 %all-gather.14.cloned.1.call-done = bf16[1024,672]{0,1:T(8,128)(2,1)} async-done(((bf16[128,672]{0,1:T(8,128)(2,1)}), bf16[1024,672]{0,1:T(8,128)(2,1)}) %all-gather.14.cloned.1.call-update) | async-done | bytes 1376272 | tf_op jit(solution)/shard_map/all_gather | solution.py:41
  358.5 0.0 copy-done.3
  358.6 4.0 convolution_convert_fusion
  362.6 101.8 %reduce-scatter.5.cloned.1.call-done = f32[32,1024]{1,0:T(8,128)} async-done(((f32[1024,1024]{1,0:T(8,128)}), f32[32,1024]{1,0:T(8,128)}) %reduce-scatter.5.cloned.1.call-update) | async-done | bytes 131088 | tf_op jit(solution)/shard_map/reduce_scatter | solution.py:55
  464.4 1.5 convert_element_type.29
Async XLA Ops:
  7.2 61.0 %copy-start = (bf16[672,1024]{1,0:T(8,128)(2,1)S(1)}, bf16[672,1024]{1,0:T(8,128)(2,1)}, u32[]{:S(2)}) copy-start(bf16[672,1024]{1,0:T(8,128)(2,1)} %param.9) | copy-start | bytes 4128772
  7.2 4.1 copy-start.2
  7.2 61.0 %all-gather.8.cloned.1.call-start = ((), (), s32[]{:S(2)}) async-start(), calls=%async_computation.3 | async-start | bytes 2162688 | tf_op jit(solution)/shard_map/all_gather | solution.py:23
  7.9 114.5 %all-gather.6.cloned.1.call-start = ((), (), s32[]{:S(2)}) async-start(), calls=%async_computation.2 | async-start | bytes 2162688 | tf_op jit(solution)/shard_map/all_gather | solution.py:22
  8.7 213.3 %reduce-scatter.3.cloned.1.call-start = ((), (), s32[]{:S(2)}) async-start(), calls=%async_computation.4 | async-start | bytes 9289728 | tf_op jit(solution)/shard_map/reduce_scatter | solution.py:33
  122.4 5.6 %copy-start.1 = (f32[1024,672]{0,1:T(8,128)S(1)}, f32[1024,672]{0,1:T(8,128)}, u32[]{:S(2)}) copy-start(f32[1024,672]{0,1:T(8,128)} %fusion.7) | copy-start | bytes 8257540
  133.0 134.2 %all-gather.10.cloned.1.call-start = ((), (), s32[]{:S(2)}) async-start(), calls=%async_computation.5 | async-start | bytes 1548288 | tf_op jit(solution)/shard_map/all_gather | solution.py:42
  224.2 88.7 %all-gather.12.cloned.1.call-start = ((), (), s32[]{:S(2)}) async-start(), calls=%async_computation.6 | async-start | bytes 1548288 | tf_op jit(solution)/shard_map/all_gather | solution.py:43
  224.8 133.8 %all-gather.14.cloned.1.call-start = ((), (), s32[]{:S(2)}) async-start(), calls=%async_computation.8 | async-start | bytes 1548288 | tf_op jit(solution)/shard_map/all_gather | solution.py:41
  225.3 239.0 %reduce-scatter.5.cloned.1.call-start = ((), (), s32[]{:S(2)}) async-start(), calls=%async_computation.7 | async-start | bytes 4325376 | tf_op jit(solution)/shard_map/reduce_scatter | solution.py:55
  321.0 1.6 copy-start.4
  322.6 4.2 copy-start.5
  322.6 4.2 copy-start.6
  326.8 31.8 %copy-start.3 = (bf16[1024,1024]{1,0:T(8,128)(2,1)S(1)}, bf16[1024,1024]{1,0:T(8,128)(2,1)}, u32[]{:S(2)}) copy-start(bf16[1024,1024]{1,0:T(8,128)(2,1)} %all-gather.8.cloned.1.call-done) | copy-start | bytes 6291460
Sparse Core Ops, SparseCore 0:
  10.6 57.5 all-gather.7
  70.7 51.6 all-gather.5
  133.1 88.8 reduce-scatter.2
  224.3 42.8 all-gather.9
  269.4 43.3 all-gather.11
  315.1 43.3 all-gather.13
  363.0 101.3 reduce-scatter.4
where the time goes:
time: 473 us
  waiting for transfers between devices  415 us (88%)
  matrix products  29.4 us (6%)
  between operations  14.2 us (3%)
  other arithmetic  8.58 us (2%)
  local copies, waits for them, and re-layouts  5.38 us (1%)
    reduce_scatter x1, waiting for transfers between devices, per_device(): lax.psum_scatter(lax.dot_general(both_deltas, both_weights, contract_cols...  102 us
    reduce_scatter x1, waiting for transfers between devices, per_device(): lax.psum_scatter(jnp.concatenate([forward_part, backward_part], axis=1),...  89 us
    all_gather x1, waiting for transfers between devices, per_device(): lax.all_gather(cotangent, 'col', axis=0, tiled=True)  55.7 us
    all_gather x1, waiting for transfers between devices, per_device(): lax.all_gather(activations, 'col', axis=0, tiled=True)  49.5 us
    all_gather x1, waiting for transfers between devices, per_device(): lax.all_gather(up_delta, 'row', axis=0, tiled=True)  45.7 us
    all_gather x1, waiting for transfers between devices, per_device(): lax.all_gather(gate_delta, 'row', axis=0, tiled=True)  41.6 us
    all_gather x1, waiting for transfers between devices, per_device(): lax.all_gather(hidden, 'row', axis=0, tiled=True)  29.1 us
  transfers between devices with their start and end apart: 7, of which 7 were waited for; matrix products, arithmetic and copies ran while one was open for 6% of the time, Pallas kernels for 0%

commit v1 on v0

--- a/solution.py
+++ b/solution.py
@@ -20,7 +20,9 @@
 def per_device(activations, cotangent, gate_weight, up_weight, down_weight):
     act_all, cot_all = (
         lax.all_gather(activations, "col", axis=0, tiled=True),
-        lax.all_gather(cotangent, "col", axis=0, tiled=True),
+        jnp.concatenate(
+            lax.all_to_all(jnp.stack([cotangent] * lax.axis_size("col")), "col", 0, 0), axis=0
+        ),
     )
     hid_cols = gate_weight.shape[1]
     both_weights = jnp.concatenate([gate_weight, up_weight], axis=1)

time: 473 us -> 439 us (0.928)
  waiting for transfers between devices: 415 us -> 370 us
  starting transfers between devices: 0.45 us -> 11.7 us
    all_gather x1 -> x0, waiting for transfers between devices: 55.7 us -> none  [per_device(): lax.all_gather(cotangent, 'col', axis=0, tiled=True)]
    all_to_all x0 -> x1, waiting for transfers between devices: none -> 49 us  [per_device(): lax.all_to_all(jnp.stack([cotangent] * lax.axis_size('col')), 'col', 0, 0)]
    all_gather x1, waiting for transfers between devices: 49.5 us -> 10.4 us  [per_device(): lax.all_gather(activations, 'col', axis=0, tiled=True)]
    all_to_all x0 -> x1, starting transfers between devices: none -> 11.3 us  [per_device(): lax.all_to_all(jnp.stack([cotangent] * lax.axis_size('col')), 'col', 0, 0)]
where the time goes in v1:
time: 439 us
  waiting for transfers between devices  370 us (84%)
  matrix products  28.4 us (6%)
  between operations  14.2 us (3%)
  starting transfers between devices  11.7 us (3%)
  other arithmetic  8.56 us (2%)
  local copies, waits for them, and re-layouts  6.43 us (1%)
    reduce_scatter x1, waiting for transfers between devices, per_device(): lax.psum_scatter(lax.dot_general(both_deltas, both_weights, contract_cols...  102 us
    reduce_scatter x1, waiting for transfers between devices, per_device(): lax.psum_scatter(jnp.concatenate([forward_part, backward_part], axis=1),...  89.4 us
    all_to_all x1, waiting for transfers between devices, per_device(): lax.all_to_all(jnp.stack([cotangent] * lax.axis_size('col')), 'col', 0, 0)  49 us
    all_gather x1, waiting for transfers between devices, per_device(): lax.all_gather(up_delta, 'row', axis=0, tiled=True)  45.7 us
    all_gather x1, waiting for transfers between devices, per_device(): lax.all_gather(gate_delta, 'row', axis=0, tiled=True)  41.8 us
    all_gather x1, waiting for transfers between devices, per_device(): lax.all_gather(hidden, 'row', axis=0, tiled=True)  30 us
    all_to_all x1, starting transfers between devices, per_device(): lax.all_to_all(jnp.stack([cotangent] * lax.axis_size('col')), 'col', 0, 0)  11.3 us
    all_gather x1, waiting for transfers between devices, per_device(): lax.all_gather(activations, 'col', axis=0, tiled=True)  10.4 us
  transfers between devices with their start and end apart: 7, of which 7 were waited for; matrix products, arithmetic and copies ran while one was open for 6% of the time, Pallas kernels for 0%

profile of v1, /device:TPU:8, one launch (start us, length us, event | category | flops | bytes accessed | tf_op | source)
XLA Modules:
  0.0 439.0 jit_solution(16829743270430711331)
XLA Ops:
  7.2 0.0 copy-start
  7.2 2.6 stack.2
  9.7 11.3 %all-to-all-start = ((bf16[32,32,1024]{2,1,0:T(8,128)(2,1)}), bf16[32,32,1024]{2,1,0:T(8,128)(2,1)S(1)}, u32[]{:S(2)}, u32[]{:S(2)}) async-start(bf16[32,32,1024]{2,1,0:T(8,128)(2,1)} %stack.2), calls=%async_computation | async-start | bytes 4194304 | tf_op jit(solution)/shard_map/all_to_all | solution.py:24
  21.1 0.0 all-gather.5.cloned.1.call-start
  21.1 0.7 all-gather.5.cloned.1.call-update
  21.8 0.0 reduce-scatter.3.cloned.1.call-start
  21.9 0.0 copy-start.2
  21.9 2.6 constant_dynamic-update-slice_fusion.1
  24.5 0.0 copy-done.2
  24.5 1.2 constant_dynamic-update-slice_fusion
  25.7 49.0 %all-to-all-done = bf16[32,32,1024]{2,1,0:T(8,128)(2,1)S(1)} async-done(((bf16[32,32,1024]{2,1,0:T(8,128)(2,1)}), bf16[32,32,1024]{2,1,0:T(8,128)(2,1)S(1)}, u32[]{:S(2)}, u32[]{:S(2)}) %all-to-all-start) | async-done | bytes 2097184 | tf_op jit(solution)/shard_map/all_to_all | solution.py:24
  74.7 0.0 copy-done
  74.7 3.2 fusion.7
  77.8 10.4 %all-gather.5.cloned.1.call-done = bf16[1024,1024]{1,0:T(8,128)(2,1)} async-done(((bf16[32,1024]{1,0:T(8,128)(2,1)}), bf16[1024,1024]{1,0:T(8,128)(2,1)}) %all-gather.5.cloned.1.call-update) | async-done | bytes 2097168 | tf_op jit(solution)/shard_map/all_gather | solution.py:22
  88.2 0.0 copy-start.1
  88.2 5.6 %convolution_bitcast_fusion = f32[1024,1344]{0,1:T(8,128)S(1)} fusion(bf16[1024,1344]{0,1:T(8,128)(2,1)} %constant_dynamic-update-slice_fusion, bf16[1024,1024]{1,0:T(8,128)(2,1)} %all-gather.5.cloned.1.call-done), kind=kOutput, calls=%fused_computation.1 | convolution fusion | flops 2818572288 | bytes 10354688 | tf_op jit(solution)/shard_map/dot_general | solution.py:31
  93.9 0.0 copy-done.1
  93.9 4.9 %pad_maximum_fusion = f32[1024,2016]{0,1:T(8,128)} fusion(f32[1024,672]{0,1:T(8,128)S(1)} %copy-done.1, f32[1024,1344]{0,1:T(8,128)S(1)} %convolution_bitcast_fusion), kind=kLoop, calls=%fused_computation | loop fusion | flops 2064384 | bytes 16515072 | tf_op jit(solution)/shard_map/concatenate | solution.py:36
  98.8 0.0 reduce-scatter.3.cloned.1.call-update
  98.8 0.0 all-gather.7.cloned.1.call-start
  98.8 89.4 %reduce-scatter.3.cloned.1.call-done = f32[128,2016]{0,1:T(8,128)} async-done(((f32[1024,2016]{0,1:T(8,128)}), f32[128,2016]{0,1:T(8,128)}) %reduce-scatter.3.cloned.1.call-update) | async-done | bytes 1032208 | tf_op jit(solution)/shard_map/reduce_scatter | solution.py:35
  188.2 2.1 multiply_convert_fusion
  190.4 0.0 all-gather.7.cloned.1.call-update
  190.4 0.0 all-gather.9.cloned.1.call-start
  190.4 0.5 all-gather.9.cloned.1.call-update
  191.0 0.0 all-gather.11.cloned.1.call-start
  191.0 0.5 all-gather.11.cloned.1.call-update
  191.5 0.2 reduce-scatter.5.cloned.1.call-start
  191.8 41.8 %all-gather.7.cloned.1.call-done = bf16[1024,672]{0,1:T(8,128)(2,1)} async-done(((bf16[128,672]{0,1:T(8,128)(2,1)}), bf16[1024,672]{0,1:T(8,128)(2,1)}) %all-gather.7.cloned.1.call-update) | async-done | bytes 1376272 | tf_op jit(solution)/shard_map/all_gather | solution.py:44
  233.5 45.7 %all-gather.9.cloned.1.call-done = bf16[1024,672]{0,1:T(8,128)(2,1)} async-done(((bf16[128,672]{0,1:T(8,128)(2,1)}), bf16[1024,672]{0,1:T(8,128)(2,1)}) %all-gather.9.cloned.1.call-update) | async-done | bytes 1376272 | tf_op jit(solution)/shard_map/all_gather | solution.py:45
  279.2 8.1 %fusion = f32[1024,1024]{1,0:T(8,128)} fusion(bf16[1024,1344]{0,1:T(8,128)(2,1)} %constant_dynamic-update-slice_fusion, bf16[1024,672]{0,1:T(8,128)(2,1)} %all-gather.9.cloned.1.call-done, bf16[1024,672]{0,1:T(8,128)(2,1)} %all-gather.7.cloned.1.call-done), kind=kOutput, calls=%fused_computation.2 | convolution fusion | flops 2824077312 | bytes 9699328 | tf_op jit(solution)/shard_map/dot_general | solution.py:58
  287.4 0.0 reduce-scatter.5.cloned.1.call-update
  287.4 0.0 copy-start.3
  287.4 0.0 copy-start.4
  287.4 4.8 %fusion.5 = bf16[1024,672]{0,1:T(8,128)(2,1)} fusion(bf16[1024,672]{0,1:T(8,128)(2,1)} %all-gather.9.cloned.1.call-done, bf16[1024,1024]{1,0:T(8,128)(2,1)} %all-gather.5.cloned.1.call-done), kind=kOutput, calls=%fused_computation.10 | convolution fusion | flops 1409974272 | bytes 4849664 | tf_op jit(solution)/shard_map/dot_general | solution.py:53
  292.2 0.0 copy-done.3
  292.2 0.0 copy-done.4
  292.2 2.7 fusion.4
  294.9 30.0 %all-gather.11.cloned.1.call-done = bf16[1024,672]{0,1:T(8,128)(2,1)} async-done(((bf16[128,672]{0,1:T(8,128)(2,1)}), bf16[1024,672]{0,1:T(8,128)(2,1)}) %all-gather.11.cloned.1.call-update) | async-done | bytes 1376272 | tf_op jit(solution)/shard_map/all_gather | solution.py:43
  324.9 4.0 convolution_convert_fusion
  328.9 101.6 %reduce-scatter.5.cloned.1.call-done = f32[32,1024]{1,0:T(8,128)} async-done(((f32[1024,1024]{1,0:T(8,128)}), f32[32,1024]{1,0:T(8,128)}) %reduce-scatter.5.cloned.1.call-update) | async-done | bytes 131088 | tf_op jit(solution)/shard_map/reduce_scatter | solution.py:57
  430.6 1.5 convert_element_type.29
Async XLA Ops:
  7.2 67.5 %copy-start = (bf16[672,1024]{1,0:T(8,128)(2,1)S(1)}, bf16[672,1024]{1,0:T(8,128)(2,1)}, u32[]{:S(2)}) copy-start(bf16[672,1024]{1,0:T(8,128)(2,1)} %param.9) | copy-start | bytes 4128772
  9.7 64.9 %all-to-all-start = ((bf16[32,32,1024]{2,1,0:T(8,128)(2,1)}), bf16[32,32,1024]{2,1,0:T(8,128)(2,1)S(1)}, u32[]{:S(2)}, u32[]{:S(2)}) async-start(bf16[32,32,1024]{2,1,0:T(8,128)(2,1)} %stack.2), calls=%async_computation | async-start | bytes 4194304 | tf_op jit(solution)/shard_map/all_to_all | solution.py:24
  21.1 67.2 %all-gather.5.cloned.1.call-start = ((), (), s32[]{:S(2)}) async-start(), calls=%async_computation.3 | async-start | bytes 2162688 | tf_op jit(solution)/shard_map/all_gather | solution.py:22
  21.8 166.4 %reduce-scatter.3.cloned.1.call-start = ((), (), s32[]{:S(2)}) async-start(), calls=%async_computation.4 | async-start | bytes 9289728 | tf_op jit(solution)/shard_map/reduce_scatter | solution.py:35
  21.9 2.6 copy-start.2
  88.2 5.6 %copy-start.1 = (f32[1024,672]{0,1:T(8,128)S(1)}, f32[1024,672]{0,1:T(8,128)}, u32[]{:S(2)}) copy-start(f32[1024,672]{0,1:T(8,128)} %fusion.7) | copy-start | bytes 8257540
  98.8 134.8 %all-gather.7.cloned.1.call-start = ((), (), s32[]{:S(2)}) async-start(), calls=%async_computation.5 | async-start | bytes 1548288 | tf_op jit(solution)/shard_map/all_gather | solution.py:44
  190.4 88.9 %all-gather.9.cloned.1.call-start = ((), (), s32[]{:S(2)}) async-start(), calls=%async_computation.6 | async-start | bytes 1548288 | tf_op jit(solution)/shard_map/all_gather | solution.py:45
  191.0 134.0 %all-gather.11.cloned.1.call-start = ((), (), s32[]{:S(2)}) async-start(), calls=%async_computation.8 | async-start | bytes 1548288 | tf_op jit(solution)/shard_map/all_gather | solution.py:43
  191.5 239.0 %reduce-scatter.5.cloned.1.call-start = ((), (), s32[]{:S(2)}) async-start(), calls=%async_computation.7 | async-start | bytes 4325376 | tf_op jit(solution)/shard_map/reduce_scatter | solution.py:57
  287.4 4.8 %copy-start.3 = (bf16[1024,1024]{1,0:T(8,128)(2,1)S(1)}, bf16[1024,1024]{1,0:T(8,128)(2,1)}, u32[]{:S(2)}) copy-start(bf16[1024,1024]{1,0:T(8,128)(2,1)} %all-gather.5.cloned.1.call-done) | copy-start | bytes 6291460
  287.4 4.8 %copy-start.4 = (bf16[1024,672]{0,1:T(8,128)(2,1)S(1)}, bf16[1024,672]{0,1:T(8,128)(2,1)}, u32[]{:S(2)}) copy-start(bf16[1024,672]{0,1:T(8,128)(2,1)} %all-gather.7.cloned.1.call-done) | copy-start | bytes 4128772
Sparse Core Ops, SparseCore 0:
  24.5 63.7 all-gather.4
  98.9 89.2 reduce-scatter.2
  190.6 42.8 all-gather.6
  235.8 43.3 all-gather.8
  281.5 43.3 all-gather.10
  329.2 101.3 reduce-scatter.4
